TPU v7x, 32 devices: a whole 2x2x4 slice. The times are simulated.
32 devices in a mesh: seq: 8 (over y, x, core), tp: 4 (over z).
Axes of the slice: x: 2, y: 2, z: 4, core: 2. Of those that a mesh axis runs over, the one named last changes fastest.
Arguments:
- hidden_in: bfloat16 [2048, 4096], P('seq', 'tp'), may hold values from -6 to 6
- order: int32 [2048], P('seq'), may hold values from 0 to 2047, as said below
- segment: int32 [2048], replicated, may hold values from 0 to 3, never falling along the last dimension, each value on 1 to 1024 neighbouring positions
- norm_gain: float32 [4096], replicated, may hold values from 0.1 to 1.9
- w_query: bfloat16 [4096, 2048], P('seq', 'tp')
- w_key: bfloat16 [4096, 512], P('seq', 'tp'), may hold values from -0.09375 to 0.09375
- w_value: bfloat16 [4096, 512], P('seq', 'tp'), may hold values from -0.09375 to 0.09375
- w_out: bfloat16 [2048, 4096], P('seq', 'tp'), may hold values from -0.5 to 0.5
Outputs:
- attn_out: bfloat16 [2048, 4096], P('seq', 'tp')
Inputs may be any that keep to these rules, and one draw needn't show every extreme that they name: order holds every position once; it is made of runs of 64 consecutive positions, each starting at a multiple of 64 and stored in rows that start at a multiple of 64. `segment`: never falls along positions.
All inputs are finite; a program needn't handle non-finite values.
Results may differ from a plain program's by a relative error of at most 0.014.
The roundings to bfloat16 on the way count: a program that leaves them out, or rounds other values in their place, can miss the bound.
Values may be sent and summed in bfloat16 or wider, within the bound.
A program may use at most 128 MiB of HBM per device.

v0:
```python
import jax
import jax.numpy as jnp
from jax import lax
from jax.sharding import PartitionSpec as P

HD = 128


THETA = 500000.0
EPS = 1e-05


def rotary(block, positions):
    head_dim = block.shape[-1]
    width = head_dim // 2
    frequency = THETA ** (-jnp.arange(width, dtype=jnp.float32) * 2.0 / head_dim)
    angle = positions.astype(jnp.float32)[:, None] * frequency[None, :]
    cosine = jnp.cos(angle)[:, None, :]
    sine = jnp.sin(angle)[:, None, :]
    first = block[..., :width]
    second = block[..., width:]
    return jnp.concatenate(
        [first * cosine - second * sine, second * cosine + first * sine], axis=-1
    )


def on_device(hidden_in, order, segment, norm_gain, w_query, w_key, w_value, w_out):
    rows = hidden_in.shape[0]
    whole = lax.all_gather(hidden_in, "tp", axis=1, tiled=True)
    wide = whole.astype(jnp.float32)
    mean_square = jnp.mean(wide * wide, axis=1, keepdims=True)
    normed = (wide * lax.rsqrt(mean_square + EPS) * norm_gain[None, :]).astype(jnp.bfloat16)
    pieces = (
        lax.all_gather(w_query, "seq", axis=0, tiled=True),
        lax.all_gather(w_key, "seq", axis=0, tiled=True),
        lax.all_gather(w_value, "seq", axis=0, tiled=True),
    )
    columns = normed
    query, key, value = tuple(
        (jnp.dot(columns, piece, preferred_element_type=jnp.float32) for piece in pieces)
    )
    heads_local = w_query.shape[1] // HD
    groups_local = w_key.shape[1] // HD
    group = heads_local // groups_local
    query = (rotary(query.reshape(rows, heads_local, HD), order) * HD ** (-0.5)).astype(
        jnp.bfloat16
    )
    query = query.reshape(rows, groups_local, group, HD)
    key = rotary(key.reshape(rows, groups_local, HD), order).astype(jnp.bfloat16)
    value = value.reshape(rows, groups_local, HD).astype(jnp.bfloat16)
    document = jnp.take(segment, order, axis=0)

    def attend(carry, block):
        key_block, value_block, key_order, key_document = block
        allowed = (key_order[None, :] <= order[:, None]) & (
            key_document[None, :] == document[:, None]
        )

        def compute(state):
            maximum, total, weighted = state
            scores = jnp.einsum(
                "rkgd,ckd->rkgc", query, key_block, preferred_element_type=jnp.float32
            )
            scores = jnp.where(allowed[:, None, None, :], scores, -jnp.inf)
            new_max = jnp.maximum(maximum, jnp.max(scores, axis=-1))
            anchor = jnp.where(new_max == -jnp.inf, 0.0, new_max)
            weights = jnp.exp(scores - anchor[..., None])
            shrink = jnp.exp(maximum - anchor)
            total = total * shrink + jnp.sum(weights, axis=-1)
            weighted = weighted * shrink[..., None] + jnp.einsum(
                "rkgc,ckd->rkgd",
                weights.astype(jnp.bfloat16),
                value_block,
                preferred_element_type=jnp.float32,
            )
            return (new_max, total, weighted)

        return lax.cond(jnp.any(allowed), compute, lambda state: state, carry)

    initial = (
        jnp.full((rows, groups_local, group), -jnp.inf, jnp.float32),
        jnp.zeros((rows, groups_local, group), jnp.float32),
        jnp.zeros((rows, groups_local, group, HD), jnp.float32),
    )
    carry = initial
    piece = (
        lax.all_gather(key, "seq", axis=0, tiled=True),
        lax.all_gather(value, "seq", axis=0, tiled=True),
        lax.all_gather(order, "seq", axis=0, tiled=True),
        lax.all_gather(document, "seq", axis=0, tiled=True),
    )
    count = piece[0].shape[0]
    stacked = tuple((member.reshape((count // 512, 512) + member.shape[1:]) for member in piece))
    carry, unused = lax.scan(lambda state, block: (attend(state, block), None), carry, stacked)
    maximum, total, weighted = carry
    mixed = (weighted / total[..., None]).reshape(rows, heads_local * HD).astype(jnp.bfloat16)
    every_head = lax.all_gather(mixed, "tp", axis=1, tiled=True)
    piece = lax.all_gather(w_out, "seq", axis=0, tiled=True)
    columns = every_head
    result = jnp.dot(columns, piece, preferred_element_type=jnp.float32)
    return result.astype(jnp.bfloat16)


def solution(mesh):
    placed = (
        P("seq", "tp"),
        P("seq"),
        P(),
        P(),
        P("seq", "tp"),
        P("seq", "tp"),
        P("seq", "tp"),
        P("seq", "tp"),
    )
    return jax.shard_map(
        on_device, mesh=mesh, in_specs=placed, out_specs=P("seq", "tp"), check_vma=False
    )
```

profile of v0, /device:TPU:0, one launch (start us, length us, event | category | flops | bytes accessed | tf_op | source)
XLA Modules:
  0.0 225.6 jit_solution(5742944631915950795)
XLA Ops:
  6.5 0.7 all-gather.10.cloned.1.call-update
  7.3 0.7 all-gather.12.cloned.1.call-update
  8.1 0.7 all-gather.16.cloned.1.call-update
  8.8 0.5 all-gather.14.cloned.1.call-update
  9.4 0.5 all-gather.20.cloned.1.call-update
  10.0 0.7 compare_select_fusion.1
  10.7 1.7 gather_fusion
  12.4 10.3 %all-gather.2 = s32[8,1,256]{2,1,0:T(1,128)S(1)} all-gather(s32[1,1,256]{2,1,0:T(1,128)S(1)} %bitcast.80), channel_id=1, replica_groups=mesh['seq'=8,'tp'=4] {'seq'}, dimensions={0}, use_global_device_ids=true | all-gather | bytes 9216 | tf_op jit(solution)/shard_map/all_gather | solution.py:90
  22.8 8.9 %all-gather.1 = s32[8,1,256]{2,1,0:T(1,128)S(1)} all-gather(s32[1,1,256]{2,1,0:T(1,128)S(1)} %bitcast.79), channel_id=1, replica_groups=mesh['seq'=8,'tp'=4] {'seq'}, dimensions={0}, use_global_device_ids=true | all-gather | bytes 9216 | tf_op jit(solution)/shard_map/all_gather | solution.py:89
  31.7 0.5 multiply_cosine_fusion
  32.3 25.3 %all-gather.10.cloned.1.call-done = bf16[256,4096]{1,0:T(8,128)(2,1)} async-done(((bf16[256,1024]{1,0:T(8,128)(2,1)}), bf16[256,4096]{1,0:T(8,128)(2,1)}) %all-gather.10.cloned.1.call-update) | async-done | bytes 2097168 | tf_op jit(solution)/shard_map/all_gather | solution.py:29
  57.6 2.2 fusion.20
  59.8 21.9 %all-gather.12.cloned.1.call-done = bf16[4096,128]{1,0:T(8,128)(2,1)} async-done(((bf16[512,128]{1,0:T(8,128)(2,1)}), bf16[4096,128]{1,0:T(8,128)(2,1)}) %all-gather.12.cloned.1.call-update) | async-done | bytes 1048592 | tf_op jit(solution)/shard_map/all_gather | solution.py:35
  81.7 2.2 convolution_bitcast_fusion.1
  84.3 12.5 %all_gather.34 = bf16[2048,1,128]{0,2,1:T(8,128)(2,1)S(1)} all-gather(bf16[256,1,128]{0,2,1:T(8,128)(2,1)S(1)} %pad_maximum_fusion), channel_id=1, replica_groups=mesh['seq'=8,'tp'=4] {'seq'}, dimensions={0}, use_global_device_ids=true | all-gather | bytes 589824 | tf_op jit(solution)/shard_map/all_gather | solution.py:87
  97.0 10.8 %all-gather.16.cloned.1.call-done = bf16[4096,128]{1,0:T(8,128)(2,1)} async-done(((bf16[512,128]{1,0:T(8,128)(2,1)}), bf16[4096,128]{1,0:T(8,128)(2,1)}) %all-gather.16.cloned.1.call-update) | async-done | bytes 1048592 | tf_op jit(solution)/shard_map/all_gather | solution.py:36
  107.8 2.0 convolution_convert_fusion.1
  109.8 10.8 %all-gather = bf16[2048,128]{1,0:T(8,128)(2,1)} all-gather(bf16[256,128]{1,0:T(8,128)(2,1)S(1)} %convolution_convert_fusion.1), channel_id=2, replica_groups=mesh['seq'=8,'tp'=4] {'seq'}, dimensions={0}, use_global_device_ids=true | all-gather | bytes 589824 | tf_op jit(solution)/shard_map/all_gather | solution.py:88
  120.6 1.2 copy.23
  121.8 24.4 %all-gather.14.cloned.1.call-done = bf16[4096,512]{1,0:T(8,128)(2,1)} async-done(((bf16[512,512]{1,0:T(8,128)(2,1)}), bf16[4096,512]{1,0:T(8,128)(2,1)}) %all-gather.14.cloned.1.call-update) | async-done | bytes 4194320 | tf_op jit(solution)/shard_map/all_gather | solution.py:34
  146.2 4.3 %fusion.33 = f32[256,512]{1,0:T(8,128)} fusion(bf16[4096,512]{1,0:T(8,128)(2,1)} %all-gather.14.cloned.1.call-done, bf16[256,4096]{1,0:T(8,128)(2,1)S(1)} %copy-done.1, f32[4096]{0:T(1024)S(1)} %copy-done.3, f32[256]{0:T(256)S(1)} %add_rsqrt_fusion), kind=kOutput, calls=%fused_computation.61 | convolution fusion | flops 1077936128 | bytes 6833152 | tf_op jit(solution)/shard_map/dot_general | solution.py:40
  150.5 1.2 reshape.252
  151.7 0.3 fusion.37
  152.5 12.7 %while.14 = (s32[]{:T(128)}, f32[256,1,4]{0,2,1:T(4,128)S(1)}, f32[256,1,4]{0,2,1:T(4,128)S(1)}, f32[256,1,4,128]{0,3,2,1:T(8,128)S(1)}, s32[4,512]{1,0:T(4,128)...) while((s32[]{:T(128)}, f32[256,1,4]{0,2,1:T(4,128)S(1)}, ...), condition=%wide.region_7.8_spmd, body=%wide.region_1.7_spmd.sunk | while | flops 273425408 | bytes 8476927 | solution.py:94
  152.5 0.8 fusion.45
  154.0 1.6 conditional.2
  154.0 0.5 fusion
  154.5 0.7 fusion.3
  155.2 0.4 fusion.2
  155.7 0.8 fusion.45
  157.2 1.6 conditional.2
  157.2 0.5 fusion
  157.7 0.7 fusion.3
  158.4 0.4 fusion.2
  158.9 0.8 fusion.45
  160.3 1.6 conditional.2
  160.4 0.5 fusion
  160.8 0.7 fusion.3
  161.6 0.4 fusion.2
  162.0 0.8 fusion.45
  163.5 1.6 conditional.2
  163.5 0.5 fusion
  164.0 0.7 fusion.3
  164.7 0.4 fusion.2
  165.2 0.7 divide_convert_fusion
  165.9 18.8 %all-gather.20.cloned.1.call-done = bf16[2048,1024]{1,0:T(8,128)(2,1)} async-done(((bf16[256,1024]{1,0:T(8,128)(2,1)}), bf16[2048,1024]{1,0:T(8,128)(2,1)}) %all-gather.20.cloned.1.call-update) | async-done | bytes 4194320 | tf_op jit(solution)/shard_map/all_gather | solution.py:98
  184.8 29.4 %all-gather.18.cloned.1.call-done = bf16[256,2048]{0,1:T(8,128)(2,1)} async-done(((bf16[256,512]{0,1:T(8,128)(2,1)}), bf16[256,2048]{0,1:T(8,128)(2,1)}) %all-gather.18.cloned.1.call-update) | async-done | bytes 1048592 | tf_op jit(solution)/shard_map/all_gather | solution.py:97
  214.1 4.6 %convolution_convert_fusion = bf16[256,1024]{1,0:T(8,128)(2,1)} fusion(bf16[256,2048]{0,1:T(8,128)(2,1)} %all-gather.18.cloned.1.call-done, bf16[2048,1024]{1,0:T(8,128)(2,1)} %all-gather.20.cloned.1.call-done), kind=kOutput, calls=%fused_computation.35 | convolution fusion | flops 1074003968 | bytes 5767168 | tf_op jit(solution)/shard_map/dot_general | solution.py:100
  (51 shorter events, 1.5 us)
Async XLA Ops:
  6.5 4.1 %copy-start = (s32[2048]{0:T(1024)S(1)}, s32[2048]{0:T(1024)}, u32[]{:S(2)}) copy-start(s32[2048]{0:T(1024)} %param.14) | copy-start | bytes 24580
  6.5 5.9 %copy-start.2 = (s32[256]{0:T(256)S(1)}, s32[256]{0:T(256)}, u32[]{:S(2)}) copy-start(s32[256]{0:T(256)} %param.13) | copy-start | bytes 3076
  6.5 51.1 %all-gather.10.cloned.1.call-start = ((), (), s32[]{:S(2)}) async-start(), calls=%async_computation | async-start | bytes 2621440 | tf_op jit(solution)/shard_map/all_gather | solution.py:29
  7.3 74.5 %all-gather.12.cloned.1.call-start = ((), (), s32[]{:S(2)}) async-start(), calls=%async_computation.1 | async-start | bytes 1179648 | tf_op jit(solution)/shard_map/all_gather | solution.py:35
  8.0 99.7 %all-gather.16.cloned.1.call-start = ((), (), s32[]{:S(2)}) async-start(), calls=%async_computation.3 | async-start | bytes 1179648 | tf_op jit(solution)/shard_map/all_gather | solution.py:36
  8.7 137.5 %all-gather.14.cloned.1.call-start = ((), (), s32[]{:S(2)}) async-start(), calls=%async_computation.2 | async-start | bytes 4718592 | tf_op jit(solution)/shard_map/all_gather | solution.py:34
  9.3 72.4 %copy-start.3 = (f32[4096]{0:T(1024)S(1)}, f32[4096]{0:T(1024)}, u32[]{:S(2)}) copy-start(f32[4096]{0:T(1024)} %param.15) | copy-start | bytes 49156
  9.3 175.4 %all-gather.20.cloned.1.call-start = ((), (), s32[]{:S(2)}) async-start(), calls=%async_computation.5 | async-start | bytes 4718592 | tf_op jit(solution)/shard_map/all_gather | solution.py:98
  9.9 204.2 %all-gather.18.cloned.1.call-start = ((), (), s32[]{:S(2)}) async-start(), calls=%async_computation.4 | async-start | bytes 1310720 | tf_op jit(solution)/shard_map/all_gather | solution.py:97
  57.6 24.1 %copy-start.1 = (bf16[256,4096]{1,0:T(8,128)(2,1)S(1)}, bf16[256,4096]{1,0:T(8,128)(2,1)}, u32[]{:S(2)}) copy-start(bf16[256,4096]{1,0:T(8,128)(2,1)} %all-gather.10.cloned.1.call-done) | copy-start | bytes 6291460
Sparse Core Ops, SparseCore 0:
  8.9 48.6 all-gather.9
  59.5 22.1 all-gather.11
  83.6 24.0 all-gather.15
  109.5 36.6 all-gather.13
  148.0 36.7 all-gather.19
  186.2 27.9 all-gather.17
where the time goes:
time: 226 us
  waiting for transfers between devices  134 us (59%)
  blocking collectives  42.4 us (19%)
  matrix products  17.7 us (8%)
  between operations  13.6 us (6%)
  other arithmetic  10 us (4%)
  local copies, waits for them, and re-layouts  4.9 us (2%)
  loops' own time  2.91 us (1%)
    all_gather x1, waiting for transfers between devices, on_device(): every_head = lax.all_gather(mixed, 'tp', axis=1, tiled=True)  29.4 us
    all_gather x1, waiting for transfers between devices, on_device(): whole = lax.all_gather(hidden_in, 'tp', axis=1, tiled=True)  25.3 us
    all_gather x1, waiting for transfers between devices, on_device(): lax.all_gather(w_query, 'seq', axis=0, tiled=True)  24.4 us
    all_gather x1, waiting for transfers between devices, on_device(): lax.all_gather(w_key, 'seq', axis=0, tiled=True)  21.9 us
    all_gather x1, waiting for transfers between devices, on_device(): piece = lax.all_gather(w_out, 'seq', axis=0, tiled=True)  18.8 us
    all_gather x1, blocking collectives, on_device(): lax.all_gather(key, 'seq', axis=0, tiled=True)  12.5 us
    all_gather x1, blocking collectives, on_device(): lax.all_gather(value, 'seq', axis=0, tiled=True)  10.8 us
    all_gather x1, waiting for transfers between devices, on_device(): lax.all_gather(w_value, 'seq', axis=0, tiled=True)  10.8 us
  transfers between devices with their start and end apart: 6, of which 6 were waited for; matrix products, arithmetic and copies ran while one was open for 12% of the time, Pallas kernels for 0%

commit v1 on v0

v1 whole, which is shorter than its diff:
```python
import functools

import numpy as np
import jax
import jax.numpy as jnp
from jax import lax
from jax.experimental import pallas as pl
from jax.experimental.pallas import tpu as pltpu
from jax.sharding import PartitionSpec as P

HD = 128
THETA = 500000.0
EPS = 1e-05
BIG = 3.0e38
MESH = pl.DeviceIdType.MESH


def flip(index, mask):
    bit = 1
    out = index
    while bit <= mask:
        if mask & bit:
            out = out + bit * (1 - 2 * ((index // bit) % 2))
        bit *= 2
    return out


class SeqGather:
    def __init__(self, buf, block, size, send, recv):
        self.buf, self.block, self.size, self.send, self.recv = buf, block, size, send, recv
        self.me = lax.axis_index("seq")
        high = []
        bit = 2
        while bit < size:
            high.append(bit)
            bit *= 2
        self.orders = (high + [1], high[::-1] + [1])

    def rows(self, j, half):
        part = self.block // 2
        start = pl.multiple_of(flip(self.me, j) * self.block + half * part, 16)
        return self.buf.at[pl.ds(start, part)]

    def copy(self, j, half, bit):
        k = self.orders[half].index(bit)
        view = self.rows(j, half)
        return pltpu.make_async_remote_copy(
            src_ref=view,
            dst_ref=view,
            send_sem=self.send.at[half, j, k],
            recv_sem=self.recv.at[half, j ^ bit],
            device_id={"seq": flip(self.me, bit)},
            device_id_type=MESH,
        )

    def last(self, j, half):
        found = -1
        for r, bit in enumerate(self.orders[half]):
            if j & bit:
                found = r
        return found

    def arrived(self, j, half):
        bit = self.orders[half][self.last(j, half)]
        view = self.rows(j, half)
        pltpu.make_async_remote_copy(
            src_ref=view,
            dst_ref=view,
            send_sem=self.send.at[half, j ^ bit, self.last(j, half)],
            recv_sem=self.recv.at[half, j],
            device_id={"seq": flip(self.me, bit)},
            device_id_type=MESH,
        ).wait_recv()

    def begin(self):
        count = len(self.orders[0])
        for k in range(count):
            for half in (0, 1):
                self.copy(0, half, self.orders[half][k]).start()

    def step(self, j, half):
        self.arrived(j, half)
        for bit in self.orders[half][self.last(j, half) + 1 :]:
            self.copy(j, half, bit).start()

    def steps(self):
        todo = [(self.last(j, half), j, half) for j in range(1, self.size) for half in (0, 1)]
        todo.sort(key=lambda item: (item[0], bin(item[1]).count("1"), item[1], item[2]))
        return [functools.partial(self.step, j, half) for _, j, half in todo]

    def finish(self):
        for half in (0, 1):
            for j in range(self.size):
                for bit in self.orders[half][self.last(j, half) + 1 :]:
                    self.copy(j, half, bit).wait_send()


class LineGather:
    def __init__(self, view, pieces, size, send, recv):
        self.view, self.pieces, self.size, self.send, self.recv = view, pieces, size, send, recv
        self.me = lax.axis_index("tp")

    def copy(self, owner, piece, way):
        view = self.view(owner, piece)
        to = self.me + 1 if way == 0 else self.me - 1
        return pltpu.make_async_remote_copy(
            src_ref=view,
            dst_ref=view,
            send_sem=self.send.at[way, owner, piece],
            recv_sem=self.recv.at[owner, piece],
            device_id={"tp": to},
            device_id_type=MESH,
        )

    def can(self, way):
        return self.me < self.size - 1 if way == 0 else self.me > 0

    def begin(self, piece):
        for way in (0, 1):

            @pl.when(self.can(way))
            def _():
                self.copy(self.me, piece, way).start()

    def step(self, k, piece, use=None):
        for way in (0, 1):
            owner = self.me - k if way == 0 else self.me + k
            here = owner >= 0 if way == 0 else owner < self.size
            source = 1 - way

            @pl.when(here)
            def _():
                view = self.view(owner, piece)
                pltpu.make_async_remote_copy(
                    src_ref=view,
                    dst_ref=view,
                    send_sem=self.send.at[way, owner, piece],
                    recv_sem=self.recv.at[owner, piece],
                    device_id={"tp": self.me - 1 if way == 0 else self.me + 1},
                    device_id_type=MESH,
                ).wait_recv()

                @pl.when(self.can(way))
                def _():
                    self.copy(owner, piece, way).start()

        if use is not None:
            for way in (0, 1):
                owner = self.me - k if way == 0 else self.me + k
                here = owner >= 0 if way == 0 else owner < self.size

                @pl.when(here)
                def _():
                    use(owner, piece)

    def finish(self):
        for piece in range(self.pieces):
            for way in (0, 1):
                for k in range(self.size):
                    owner = self.me - k if way == 0 else self.me + k
                    here = owner >= 0 if way == 0 else owner < self.size

                    @pl.when(here & self.can(way))
                    def _():
                        self.copy(owner, piece, way).wait_send()


def layer(
    seq,
    tp,
    hidden,
    order_col,
    order_row,
    segment,
    gain,
    frequency,
    w_query,
    w_key,
    w_value,
    w_out,
    out,
    x_all,
    normed,
    w_all,
    o_all,
    kv_all,
    ord_all,
    cap,
    att,
    squares,
    qkv,
    cosine,
    sine,
    local,
    x_send,
    x_recv,
    a_send,
    a_recv,
    w_send,
    w_recv,
    o_send,
    o_recv,
    k_send,
    k_recv,
    p_send,
    p_recv,
):
    me = lax.axis_index("seq")
    mine = lax.axis_index("tp")
    rows = hidden.shape[0]
    width = hidden.shape[1]
    depth = w_query.shape[0]
    q_cols = w_query.shape[1]
    k_cols = w_key.shape[1]
    o_depth = w_out.shape[0]
    tokens = kv_all.shape[0]
    heads = q_cols // HD
    groups = k_cols // HD
    group = heads // groups

    own_w = pl.ds(pl.multiple_of(me * depth, 16), depth)
    own_o = pl.ds(pl.multiple_of(me * o_depth, 16), o_depth)
    loads = [
        pltpu.make_async_copy(hidden, x_all.at[mine], local.at[0]),
        pltpu.make_async_copy(w_query, w_all.at[own_w, pl.ds(0, q_cols)], local.at[1]),
        pltpu.make_async_copy(w_key, w_all.at[own_w, pl.ds(q_cols, k_cols)], local.at[2]),
        pltpu.make_async_copy(w_value, w_all.at[own_w, pl.ds(q_cols + k_cols, k_cols)], local.at[3]),
        pltpu.make_async_copy(w_out, o_all.at[own_o], local.at[4]),
    ]
    for load in loads:
        load.start()

    barrier = pltpu.get_barrier_semaphore()
    for away in range(1, seq):
        pl.semaphore_signal(
            barrier, inc=1, device_id={"seq": (me + away) % seq}, device_id_type=MESH
        )

    for away in range(1, tp):
        pl.semaphore_signal(
            barrier, inc=1, device_id={"tp": (mine + away) % tp}, device_id_type=MESH
        )

    ord_all[me] = jnp.broadcast_to(order_row[...], ord_all.shape[1:])
    pl.semaphore_wait(barrier, seq + tp - 2)

    half_rows = rows // 2
    xs = LineGather(
        lambda owner, piece: x_all.at[owner, pl.ds(piece * half_rows, half_rows)],
        2, tp, x_send, x_recv,
    )
    ws = SeqGather(w_all, depth, seq, w_send, w_recv)
    os_ = SeqGather(o_all, o_depth, seq, o_send, o_recv)
    ks = SeqGather(kv_all, rows, seq, k_send, k_recv)
    piece_cols = q_cols // 2
    ats = LineGather(
        lambda owner, piece: att.at[
            :, pl.ds(pl.multiple_of(owner * q_cols + piece * piece_cols, HD), piece_cols)
        ],
        2, tp, a_send, a_recv,
    )

    loads[0].wait()
    xs.begin(0)
    xs.begin(1)
    for load in loads[1:4]:
        load.wait()
    ws.begin()

    def positions(away):
        to = (me + away) % seq
        return pltpu.make_async_remote_copy(
            src_ref=ord_all.at[me],
            dst_ref=ord_all.at[me],
            send_sem=p_send.at[away],
            recv_sem=p_recv.at[away],
            device_id={"seq": to},
            device_id_type=MESH,
        )

    for away in range(1, seq):
        positions(away).start()
    loads[4].wait()

    def add_squares(owner, piece):
        where = pl.ds(piece * half_rows, half_rows)
        wide = x_all[owner, where].astype(jnp.float32)
        squares[where] += jnp.sum(wide * wide, axis=1, keepdims=True)

    squares[...] = jnp.zeros_like(squares)
    add_squares(mine, 0)
    add_squares(mine, 1)
    angle = order_col[...].astype(jnp.float32) * frequency[...]
    lane = lax.broadcasted_iota(jnp.int32, angle.shape, 1)
    cosine[...] = jnp.cos(angle)
    sine[...] = jnp.where(lane < HD // 2, -1.0, 1.0) * jnp.sin(angle)

    position = order_col[...]

    def find(block, total):
        at = pl.ds(pl.multiple_of(block * rows, HD), rows)
        index = lax.broadcasted_iota(jnp.int32, (rows, rows), 1) + block * rows
        number = jnp.broadcast_to(segment[:, at].astype(jnp.float32), (rows, rows))
        return total + jnp.sum(jnp.where(index == position, number, 0.0), axis=1, keepdims=True)

    document = lax.fori_loop(0, seq, find, jnp.zeros((rows, 1), jnp.float32))

    def before(block, total):
        at = pl.ds(pl.multiple_of(block * rows, HD), rows)
        number = jnp.broadcast_to(segment[:, at].astype(jnp.float32), (rows, rows))
        return total + jnp.sum(jnp.where(number < document, 1.0, 0.0), axis=1, keepdims=True)

    first = lax.fori_loop(0, seq, before, jnp.zeros((rows, 1), jnp.float32)).astype(jnp.int32)

    def masks():
        for away in range(1, seq):
            source = (me + seq - away) % seq
            pltpu.make_async_remote_copy(
                src_ref=ord_all.at[source],
                dst_ref=ord_all.at[source],
                send_sem=p_send.at[away],
                recv_sem=p_recv.at[away],
                device_id={"seq": source},
                device_id_type=MESH,
            ).wait_recv()

        def mask(block, carry):
            other = jnp.broadcast_to(ord_all[block][0:1], (rows, rows))
            allowed = (other <= position) & (other >= first)
            cap[:, pl.ds(pl.multiple_of(block * rows, HD), rows)] = jnp.where(allowed, BIG, -BIG)
            return carry

        lax.fori_loop(0, seq, mask, 0)

    line = [(k, piece) for k in range(1, tp) for piece in (0, 1)]
    steps = ws.steps()
    ring = [steps[: len(steps) * i // 6] for i in range(1, 7)]
    done = 0
    for i, (k, piece) in enumerate(line):
        if i < len(ring):
            last = i == len(ring) - 1
            for step in steps[done : len(ring[i])]:
                step()
            done = len(ring[i])
            if last:
                os_.begin()
        xs.step(k, piece, add_squares)
        if i == 0:
            masks()
    for step in steps[done:]:
        step()

    scale = lax.rsqrt(squares[...] * (1.0 / (tp * width)) + EPS)
    for t in range(tp):
        at = pl.ds(t * width, width)
        normed[:, at] = (x_all[t].astype(jnp.float32) * scale * gain[:, at]).astype(jnp.bfloat16)

    def rotate(block):
        return block * cosine[...] + pltpu.roll(block, HD // 2, 1) * sine[...]

    qkv[...] = jnp.dot(normed[...], w_all[...], preferred_element_type=jnp.float32)
    own_rows = pl.ds(pl.multiple_of(me * rows, 16), rows)
    for g in range(groups):
        key = qkv[:, pl.ds(q_cols + g * HD, HD)]
        kv_all[own_rows, pl.ds(g * HD, HD)] = rotate(key).astype(jnp.bfloat16)
        value = qkv[:, pl.ds(q_cols + k_cols + g * HD, HD)]
        kv_all[own_rows, pl.ds(k_cols + g * HD, HD)] = value.astype(jnp.bfloat16)
    ks.begin()
    queries = [
        (rotate(qkv[:, pl.ds(h * HD, HD)]) * HD ** (-0.5)).astype(jnp.bfloat16)
        for h in range(heads)
    ]
    for step in ks.steps():
        step()
    out_steps = os_.steps()
    early = [step for step in out_steps]

    chunk = min(tokens, 2048)
    chunks = tokens // chunk

    def part(h, start):
        g = h // group
        key = kv_all[pl.ds(start, chunk), pl.ds(g * HD, HD)]
        scores = lax.dot_general(
            queries[h], key, (((1,), (1,)), ((), ())), preferred_element_type=jnp.float32
        )
        return jnp.minimum(scores, cap[:, pl.ds(start, chunk)])

    def mix(h, start, weights):
        g = h // group
        value = kv_all[pl.ds(start, chunk), pl.ds(k_cols + g * HD, HD)]
        return jnp.dot(weights.astype(jnp.bfloat16), value, preferred_element_type=jnp.float32)

    per_piece = heads // 2
    for h in range(heads):
        scores = part(h, 0)
        top = jnp.max(scores, axis=1, keepdims=True)
        weights = jnp.exp(scores - top)
        total = jnp.sum(weights, axis=1, keepdims=True)
        weighted = mix(h, 0, weights)
        if chunks > 1:

            def more(block, state, h=h):
                top, total, weighted = state
                start = pl.multiple_of(block * chunk, HD)
                scores = part(h, start)
                higher = jnp.maximum(top, jnp.max(scores, axis=1, keepdims=True))
                shrink = jnp.exp(top - higher)
                weights = jnp.exp(scores - higher)
                total = total * shrink + jnp.sum(weights, axis=1, keepdims=True)
                return higher, total, weighted * shrink + mix(h, start, weights)

            top, total, weighted = lax.fori_loop(1, chunks, more, (top, total, weighted))
        at = pl.ds(pl.multiple_of(mine * q_cols + h * HD, HD), HD)
        att[:, at] = (weighted / total).astype(jnp.bfloat16)
        if (h + 1) % per_piece == 0:
            ats.begin((h + 1) // per_piece - 1)
        cut = [len(early) * i // heads for i in range(heads + 1)]
        for step in early[cut[h] : cut[h + 1]]:
            step()

    for k, piece in line:
        ats.step(k, piece)
    result = jnp.dot(att[...], o_all[...], preferred_element_type=jnp.float32)
    out[...] = result.astype(jnp.bfloat16)

    xs.finish()
    ats.finish()
    ws.finish()
    os_.finish()
    ks.finish()
    for away in range(1, seq):
        positions(away).wait_send()


def on_device(seq, tp, hidden_in, order, segment, norm_gain, w_query, w_key, w_value, w_out):
    rows, width = hidden_in.shape
    depth, q_cols = w_query.shape
    k_cols = w_key.shape[1]
    o_depth, o_cols = w_out.shape
    tokens = rows * seq
    half = np.float64(THETA) ** (-np.arange(HD // 2, dtype=np.float64) * 2.0 / HD)
    frequency = jnp.asarray(np.concatenate([half, half])[None, :].astype(np.float32))
    bits = max(1, (seq - 1).bit_length())
    dma = pltpu.SemaphoreType.DMA
    vmem = pl.BlockSpec(memory_space=pltpu.VMEM)
    away = pl.BlockSpec(memory_space=pl.ANY)
    flops = 2 * rows * (tp * width * (q_cols + 2 * k_cols) + tp * q_cols * o_cols)
    flops += 4 * rows * tokens * q_cols
    return pl.pallas_call(
        functools.partial(layer, seq, tp),
        out_shape=jax.ShapeDtypeStruct((rows, o_cols), jnp.bfloat16),
        in_specs=[away, vmem, vmem, vmem, vmem, vmem, away, away, away, away],
        out_specs=vmem,
        scratch_shapes=[
            pltpu.VMEM((tp, rows, width), jnp.bfloat16),
            pltpu.VMEM((rows, tp * width), jnp.bfloat16),
            pltpu.VMEM((seq * depth, q_cols + 2 * k_cols), jnp.bfloat16),
            pltpu.VMEM((seq * o_depth, o_cols), jnp.bfloat16),
            pltpu.VMEM((tokens, 2 * k_cols), jnp.bfloat16),
            pltpu.VMEM((seq, 8, rows), jnp.int32),
            pltpu.VMEM((rows, tokens), jnp.float32),
            pltpu.VMEM((rows, tp * q_cols), jnp.bfloat16),
            pltpu.VMEM((rows, 1), jnp.float32),
            pltpu.VMEM((rows, q_cols + 2 * k_cols), jnp.float32),
            pltpu.VMEM((rows, HD), jnp.float32),
            pltpu.VMEM((rows, HD), jnp.float32),
            dma((5,)),
            dma((2, tp, 2)),
            dma((tp, 2)),
            dma((2, tp, 2)),
            dma((tp, 2)),
            dma((2, seq, bits)),
            dma((2, seq)),
            dma((2, seq, bits)),
            dma((2, seq)),
            dma((2, seq, bits)),
            dma((2, seq)),
            dma((seq,)),
            dma((seq,)),
        ],
        compiler_params=pltpu.CompilerParams(
            collective_id=0, has_side_effects=True, vmem_limit_bytes=58 * 1024 * 1024
        ),
        cost_estimate=pl.CostEstimate(
            flops=flops, bytes_accessed=4 * 1024 * 1024, transcendentals=rows * tokens * q_cols // HD
        ),
    )(
        hidden_in,
        order.reshape(rows, 1),
        order.reshape(1, rows),
        segment.reshape(1, tokens),
        norm_gain.reshape(1, tp * width),
        frequency,
        w_query,
        w_key,
        w_value,
        w_out,
    )


def solution(mesh):
    placed = (
        P("seq", "tp"),
        P("seq"),
        P(),
        P(),
        P("seq", "tp"),
        P("seq", "tp"),
        P("seq", "tp"),
        P("seq", "tp"),
    )
    return jax.shard_map(
        functools.partial(on_device, mesh.shape["seq"], mesh.shape["tp"]),
        mesh=mesh,
        in_specs=placed,
        out_specs=P("seq", "tp"),
        check_vma=False,
    )
```

time: 226 us -> 93.4 us (0.41)
  waiting for transfers between devices: 134 us -> 0 us
  Pallas kernels: 0 us -> 89.9 us
  blocking collectives: 42.4 us -> 0 us
  matrix products: 17.7 us -> 0 us
  between operations: 13.6 us -> 0.01 us
  other arithmetic: 10 us -> 0 us
  loops' own time: 2.91 us -> 0 us
    all_gather x6 -> x0, waiting for transfers between devices: 131 us -> none  [the longest x1 29.4 us: on_device(): every_head = lax.all_gather(mixed, 'tp', axis=1, tiled=True)]
    pallas_call x0 -> x1, Pallas kernels: none -> 89.9 us  [on_device(): pl.pallas_call(functools.partial(layer, seq, tp), out_shape=jax.ShapeDtyp...]
    all_gather x4 -> x0, blocking collectives: 42.4 us -> none  [the longest x1 12.5 us: on_device(): lax.all_gather(key, 'seq', axis=0, tiled=True)]
    dot_general x12 -> x0, matrix products: 17.7 us -> none  [the longest x3 8.49 us: on_device(): jnp.dot(columns, piece, preferred_element_type=jnp.float32)]
    reduce_sum x5 -> x0, other arithmetic: 3.84 us -> none  [the longest x1 2.23 us: on_device(): mean_square = jnp.mean(wide * wide, axis=1, keepdims=True)]
    reduce_or x4 -> x0, other arithmetic: 3.36 us -> none  [attend(): return lax.cond(jnp.any(allowed), compute, lambda state: state, carry)]
    unnamed x6 -> x0, waiting for transfers between devices: 3.16 us -> none
    another operation x5 -> x0, loops' own time: 2.91 us -> none  [the longest x1 2.74 us: on_device(): lax.scan(lambda state, block: (attend(state, block), None), carry, stacked)]
  transfers between devices with their start and end apart: 6 -> 0, of which waited for: 6 -> 0; matrix products, arithmetic and copies ran while one was open for 12% -> 0% of each run, Pallas kernels for 0% -> 0%
where the time goes in v1:
time: 93.4 us; the launch traced here: 93.2 us
  Pallas kernels  89.9 us (96%)
  local copies, waits for them, and re-layouts  3.35 us (4%)
    pallas_call x1, Pallas kernels, on_device(): pl.pallas_call(functools.partial(layer, seq, tp), out_shape=jax.ShapeDtyp...  89.9 us
    unnamed x3, local copies, waits for them, and re-layouts  2.55 us

profile of v1, /device:TPU:0, one launch (start us, length us, event | category | flops | bytes accessed | tf_op | source)
XLA Modules:
  0.0 93.2 jit_solution(7538453385836097480)
XLA Ops:
  0.0 0.0 copy-start
  0.0 0.7 copy-done
  0.7 0.8 copy.10.order_col
  1.5 89.9 %shard_map.91 = bf16[256,1024]{1,0:T(8,128)(2,1)} custom-call(bf16[256,1024]{1,0:T(8,128)(2,1)} %hidden.1, s32[256,1]{1,0:T(8,128)} %copy.10.order_col, s32[1,256]{1,0:T(1,128)} %bitcast.4, s32[1,2048]{1,0:T(1,128)} %bitcast.7, f32[1,4096]{1,0:T(1,128)} %bitcast.6, f32[1,128]{1,0:T(1,128)} %constant.2.clone.frequency, bf16[512,512]{1,0:T(8,128)(2,1)} %w_query.1, ...), custom_call_target="tpu_custom_call" | custom-call | flops 3758096384 | bytes 4194304 | tf_op jit(solution)/shard_map/pallas_call | solution.py:450
  91.4 1.9 %copy.12 = bf16[256,1024]{1,0:T(8,128)(2,1)} copy(bf16[256,1024]{1,0:T(8,128)(2,1)} %shard_map.91) | data formatting | bytes 1048576
Async XLA Ops:
  0.0 0.7 copy-start

commit v2 on v1

--- a/solution.py
+++ b/solution.py
@@ -252,12 +252,12 @@
     ws = SeqGather(w_all, depth, seq, w_send, w_recv)
     os_ = SeqGather(o_all, o_depth, seq, o_send, o_recv)
     ks = SeqGather(kv_all, rows, seq, k_send, k_recv)
-    piece_cols = q_cols // 2
+    piece_cols = q_cols // heads
     ats = LineGather(
         lambda owner, piece: att.at[
             :, pl.ds(pl.multiple_of(owner * q_cols + piece * piece_cols, HD), piece_cols)
         ],
-        2, tp, a_send, a_recv,
+        heads, tp, a_send, a_recv,
     )
 
     loads[0].wait()
@@ -391,7 +391,7 @@
         value = kv_all[pl.ds(start, chunk), pl.ds(k_cols + g * HD, HD)]
         return jnp.dot(weights.astype(jnp.bfloat16), value, preferred_element_type=jnp.float32)
 
-    per_piece = heads // 2
+    per_piece = 1
     for h in range(heads):
         scores = part(h, 0)
         top = jnp.max(scores, axis=1, keepdims=True)
@@ -419,8 +419,9 @@
         for step in early[cut[h] : cut[h + 1]]:
             step()
 
-    for k, piece in line:
-        ats.step(k, piece)
+    for k in range(1, tp):
+        for piece in range(heads):
+            ats.step(k, piece)
     result = jnp.dot(att[...], o_all[...], preferred_element_type=jnp.float32)
     out[...] = result.astype(jnp.bfloat16)
 
@@ -468,8 +469,8 @@
             dma((5,)),
             dma((2, tp, 2)),
             dma((tp, 2)),
-            dma((2, tp, 2)),
-            dma((tp, 2)),
+            dma((2, tp, q_cols // HD)),
+            dma((tp, q_cols // HD)),
             dma((2, seq, bits)),
             dma((2, seq)),
             dma((2, seq, bits)),

time: 93.4 us -> 91.7 us (0.982)
  Pallas kernels: 89.9 us -> 88.1 us
    pallas_call x1, Pallas kernels: 89.9 us -> 88.1 us  [on_device(): pl.pallas_call(functools.partial(layer, seq, tp), out_shape=jax.ShapeDtyp...]
where the time goes in v2:
time: 91.7 us; the launch traced here: 91.5 us
  Pallas kernels  88.1 us (96%)
  local copies, waits for them, and re-layouts  3.35 us (4%)
    pallas_call x1, Pallas kernels, on_device(): pl.pallas_call(functools.partial(layer, seq, tp), out_shape=jax.ShapeDtyp...  88.1 us
    unnamed x3, local copies, waits for them, and re-layouts  2.55 us

profile of v2, /device:TPU:0, one launch (start us, length us, event | category | flops | bytes accessed | tf_op | source)
XLA Modules:
  0.0 91.5 jit_solution(13521803412157375360)
XLA Ops:
  0.0 0.0 copy-start
  0.0 0.7 copy-done
  0.7 0.8 copy.10.order_col
  1.5 88.1 %shard_map.91 = bf16[256,1024]{1,0:T(8,128)(2,1)} custom-call(bf16[256,1024]{1,0:T(8,128)(2,1)} %hidden.1, s32[256,1]{1,0:T(8,128)} %copy.10.order_col, s32[1,256]{1,0:T(1,128)} %bitcast.4, s32[1,2048]{1,0:T(1,128)} %bitcast.7, f32[1,4096]{1,0:T(1,128)} %bitcast.6, f32[1,128]{1,0:T(1,128)} %constant.2.clone.frequency, bf16[512,512]{1,0:T(8,128)(2,1)} %w_query.1, ...), custom_call_target="tpu_custom_call" | custom-call | flops 3758096384 | bytes 4194304 | tf_op jit(solution)/shard_map/pallas_call | solution.py:451
  89.6 1.9 %copy.12 = bf16[256,1024]{1,0:T(8,128)(2,1)} copy(bf16[256,1024]{1,0:T(8,128)(2,1)} %shard_map.91) | data formatting | bytes 1048576
Async XLA Ops:
  0.0 0.7 copy-start

commit v3 on v2

--- a/solution.py
+++ b/solution.py
@@ -244,10 +244,10 @@
     ord_all[me] = jnp.broadcast_to(order_row[...], ord_all.shape[1:])
     pl.semaphore_wait(barrier, seq + tp - 2)
 
-    half_rows = rows // 2
+    half_rows = rows // 4
     xs = LineGather(
         lambda owner, piece: x_all.at[owner, pl.ds(piece * half_rows, half_rows)],
-        2, tp, x_send, x_recv,
+        4, tp, x_send, x_recv,
     )
     ws = SeqGather(w_all, depth, seq, w_send, w_recv)
     os_ = SeqGather(o_all, o_depth, seq, o_send, o_recv)
@@ -261,8 +261,8 @@
     )
 
     loads[0].wait()
-    xs.begin(0)
-    xs.begin(1)
+    for piece in range(4):
+        xs.begin(piece)
     for load in loads[1:4]:
         load.wait()
     ws.begin()
@@ -288,8 +288,8 @@
         squares[where] += jnp.sum(wide * wide, axis=1, keepdims=True)
 
     squares[...] = jnp.zeros_like(squares)
-    add_squares(mine, 0)
-    add_squares(mine, 1)
+    for piece in range(4):
+        add_squares(mine, piece)
     angle = order_col[...].astype(jnp.float32) * frequency[...]
     lane = lax.broadcasted_iota(jnp.int32, angle.shape, 1)
     cosine[...] = jnp.cos(angle)
@@ -332,9 +332,9 @@
 
         lax.fori_loop(0, seq, mask, 0)
 
-    line = [(k, piece) for k in range(1, tp) for piece in (0, 1)]
+    line = [(k, piece) for k in range(1, tp) for piece in range(4)]
     steps = ws.steps()
-    ring = [steps[: len(steps) * i // 6] for i in range(1, 7)]
+    ring = [steps[: len(steps) * i // len(line)] for i in range(1, len(line) + 1)]
     done = 0
     for i, (k, piece) in enumerate(line):
         if i < len(ring):
@@ -467,8 +467,8 @@
             pltpu.VMEM((rows, HD), jnp.float32),
             pltpu.VMEM((rows, HD), jnp.float32),
             dma((5,)),
-            dma((2, tp, 2)),
-            dma((tp, 2)),
+            dma((2, tp, 4)),
+            dma((tp, 4)),
             dma((2, tp, q_cols // HD)),
             dma((tp, q_cols // HD)),
             dma((2, seq, bits)),

time: 91.7 us -> 98.2 us (1.071)
  Pallas kernels: 88.1 us -> 94.7 us
    pallas_call x1, Pallas kernels: 88.1 us -> 94.7 us  [on_device(): pl.pallas_call(functools.partial(layer, seq, tp), out_shape=jax.ShapeDtyp...]
where the time goes in v3:
time: 98.2 us; the launch traced here: 98.1 us
  Pallas kernels  94.7 us (96%)
  local copies, waits for them, and re-layouts  3.35 us (3%)
    pallas_call x1, Pallas kernels, on_device(): pl.pallas_call(functools.partial(layer, seq, tp), out_shape=jax.ShapeDtyp...  94.7 us
    unnamed x3, local copies, waits for them, and re-layouts  2.55 us

profile of v3, /device:TPU:0, one launch (start us, length us, event | category | flops | bytes accessed | tf_op | source)
XLA Modules:
  0.0 98.1 jit_solution(17034650084357876924)
XLA Ops:
  0.0 0.0 copy-start
  0.0 0.7 copy-done
  0.7 0.8 copy.10.order_col
  1.5 94.7 %shard_map.91 = bf16[256,1024]{1,0:T(8,128)(2,1)} custom-call(bf16[256,1024]{1,0:T(8,128)(2,1)} %hidden.1, s32[256,1]{1,0:T(8,128)} %copy.10.order_col, s32[1,256]{1,0:T(1,128)} %bitcast.4, s32[1,2048]{1,0:T(1,128)} %bitcast.7, f32[1,4096]{1,0:T(1,128)} %bitcast.6, f32[1,128]{1,0:T(1,128)} %constant.2.clone.frequency, bf16[512,512]{1,0:T(8,128)(2,1)} %w_query.1, ...), custom_call_target="tpu_custom_call" | custom-call | flops 3758096384 | bytes 4194304 | tf_op jit(solution)/shard_map/pallas_call | solution.py:451
  96.2 1.9 %copy.12 = bf16[256,1024]{1,0:T(8,128)(2,1)} copy(bf16[256,1024]{1,0:T(8,128)(2,1)} %shard_map.91) | data formatting | bytes 1048576
Async XLA Ops:
  0.0 0.7 copy-start
